TPU v7x, 32 devices: a whole 2x2x4 slice. The times are simulated.
32 devices in a mesh: rows: 16 (over z, x, core), grp: 2 (over y).
Axes of the slice: x: 2, y: 2, z: 4, core: 2. Of those that a mesh axis runs over, the one named last changes fastest.
Arguments:
- snapshots: float32 [131072, 256], P(('rows', 'grp'))
- blocks: bfloat16 [1024, 16, 128, 128], P(('rows', 'grp')), may hold values from -48 to 48
- columns: int32 [1024, 16], P(('rows', 'grp')), may hold values from 0 to 63
Outputs:
- projected: float32 [256, 256], replicated
- scaled_factor: float32 [256, 256], replicated
Inputs may be any that keep to these rules, and one draw needn't show every extreme that they name: `columns`: each stored block couples its block row to a block row of the same group of 2 * 32 consecutive block rows.
All inputs are finite; a program needn't handle non-finite values.
Results may differ from a plain program's by a relative error of at most 0.003.
Values may be sent and summed in bfloat16 or wider, within the bound.
A program may use at most 192 MiB of HBM per device.

v0:
```python
import functools
import math

import jax
import jax.numpy as jnp
from jax import lax
from jax.experimental import pallas as pl
from jax.experimental.pallas import tpu as pltpu
from jax.sharding import PartitionSpec as P

HIGHEST = lax.Precision.HIGHEST
LANES = 128
SUB = 8
MESH = pl.DeviceIdType.MESH


def dot(left, right, dims=((1,), (0,)), precision=HIGHEST):
    return lax.dot_general(
        left, right, (dims, ((), ())), precision=precision, preferred_element_type=jnp.float32
    )


def across(value, lane, shape):
    return jnp.broadcast_to(value[..., lane : lane + 1], shape)


def eliminate(head, tail):
    tiles = head.shape[0]
    one = (SUB, LANES)
    for tile in range(tiles):
        base = tile * SUB
        rows_h = [jnp.broadcast_to(head[tile, k : k + 1, :], one) for k in range(SUB)]
        rows_t = [jnp.broadcast_to(tail[tile, k : k + 1, :], one) for k in range(SUB)]
        d = {}
        for k in range(SUB):
            for i in range(k, SUB):
                d[k, i] = across(rows_h[k], base + i, one)
        later = tiles - tile - 1
        if later:
            rest_h = head[tile + 1 :]
            rest_t = tail[tile + 1 :]
            low = [across(rest_h, base + k, (later, SUB, LANES)) for k in range(SUB)]
        for k in range(SUB):
            scale = lax.rsqrt(d[k, k])
            for i in range(k + 1, SUB):
                d[k, i] = d[k, i] * scale
            rows_h[k] = rows_h[k] * scale
            rows_t[k] = rows_t[k] * scale
            for i in range(k + 1, SUB):
                for m in range(i, SUB):
                    d[i, m] = d[i, m] - d[k, i] * d[k, m]
                rows_h[i] = rows_h[i] - d[k, i] * rows_h[k]
                rows_t[i] = rows_t[i] - d[k, i] * rows_t[k]
            if later:
                low[k] = low[k] * scale[None]
                for m in range(k + 1, SUB):
                    low[m] = low[m] - low[k] * d[k, m][None]
                rest_h = rest_h - low[k] * rows_h[k][None]
                rest_t = rest_t - low[k] * rows_t[k][None]
            head[tile, k : k + 1, :] = rows_h[k][:1]
            tail[tile, k : k + 1, :] = rows_t[k][:1]
        if later:
            head[tile + 1 :] = rest_h
            tail[tile + 1 :] = rest_t


def factor_kernel(gram_ref, factor_ref, inverse_ref, head, tail):
    size = gram_ref.shape[0]
    n = LANES
    row = lax.broadcasted_iota(jnp.int32, (n, n), 0)
    col = lax.broadcasted_iota(jnp.int32, (n, n), 1)
    eye = jnp.where(row == col, 1.0, 0.0).astype(jnp.float32)
    tiles = (n // SUB, SUB, n)
    count = size // n

    for b in range(count):
        here = slice(b * n, (b + 1) * n)
        square = gram_ref[here, here]
        for a in range(b):
            above = factor_ref[a * n : (a + 1) * n, here]
            square = square - dot(above, above, ((0,), (0,)))
        head[...] = square.reshape(tiles)
        tail[...] = eye.reshape(tiles)
        eliminate(head, tail)
        lower = jnp.where(row >= col, tail[...].reshape(n, n), 0.0)
        factor_ref[here, here] = jnp.where(row <= col, head[...].reshape(n, n), 0.0)
        upper = lower.T
        inverse_ref[here, here] = upper
        for c in range(b + 1, count):
            there = slice(c * n, (c + 1) * n)
            rest = gram_ref[here, there]
            for a in range(b):
                span = slice(a * n, (a + 1) * n)
                rest = rest - dot(factor_ref[span, here], factor_ref[span, there], ((0,), (0,)))
            factor_ref[here, there] = dot(lower, rest)
            factor_ref[there, here] = jnp.zeros((n, n), jnp.float32)
            inverse_ref[there, here] = jnp.zeros((n, n), jnp.float32)
        for a in range(b):
            span = slice(a * n, (a + 1) * n)
            total = jnp.zeros((n, n), jnp.float32)
            for m in range(a, b):
                mid = slice(m * n, (m + 1) * n)
                total = total + dot(inverse_ref[span, mid], factor_ref[mid, here])
            inverse_ref[span, here] = -dot(total, upper)


def factorize(gram):
    size = gram.shape[0]
    square = jax.ShapeDtypeStruct((size, size), jnp.float32)
    return pl.pallas_call(
        factor_kernel,
        out_shape=(square, square),
        in_specs=[pl.BlockSpec(memory_space=pltpu.VMEM)],
        out_specs=(pl.BlockSpec(memory_space=pltpu.VMEM),) * 2,
        scratch_shapes=[pltpu.VMEM((LANES // SUB, SUB, LANES), jnp.float32)] * 2,
        compiler_params=pltpu.CompilerParams(vmem_limit_bytes=16 * 2**20),
        name="factorize",
    )(gram)


def split(value):
    high = value.astype(jnp.bfloat16)
    return high, (value - high.astype(jnp.float32)).astype(jnp.bfloat16)


def sum_kernel(axes, sizes, x_ref, out_ref, pair, own, slots, held, pair_sems, scatter_sems, gather_sems, last_sems):
    rows_axis, grp_axis = axes
    grps = sizes[1]
    chips = x_ref.shape[1]
    me_row, me_grp = lax.axis_index(rows_axis), lax.axis_index(grp_axis)
    core = lax.rem(me_row, 2)
    me = (me_row // 2) * grps + me_grp

    def chip(offset):
        other = lax.rem(me + offset, chips)
        return other, {rows_axis: (other // grps) * 2 + core, grp_axis: lax.rem(other, grps)}

    mate = {rows_axis: me_row + 1 - 2 * core, grp_axis: me_grp}

    barrier = pltpu.get_barrier_semaphore()
    pl.semaphore_signal(barrier, inc=1, device_id=mate, device_id_type=MESH)

    def greet(offset, carry):
        pl.semaphore_signal(barrier, inc=1, device_id=chip(offset)[1], device_id_type=MESH)
        return carry

    lax.fori_loop(1, chips, greet, 0)
    pl.semaphore_wait(barrier, chips)

    first = pltpu.make_async_remote_copy(
        src_ref=x_ref.at[1 - core], dst_ref=pair, send_sem=pair_sems.at[0], recv_sem=pair_sems.at[1],
        device_id=mate, device_id_type=MESH)
    first.start()
    first.wait()
    own[...] = x_ref[core] + pair[...]

    def scatter(offset):
        other, where = chip(offset)
        return pltpu.make_async_remote_copy(
            src_ref=own.at[other], dst_ref=slots.at[offset],
            send_sem=scatter_sems.at[0, offset], recv_sem=scatter_sems.at[1, offset],
            device_id=where, device_id_type=MESH)

    def gather(offset):
        _, where = chip(offset)
        return pltpu.make_async_remote_copy(
            src_ref=held.at[core, me], dst_ref=held.at[core, me],
            send_sem=gather_sems.at[0, offset], recv_sem=gather_sems.at[1, offset],
            device_id=where, device_id_type=MESH)

    def each(make, act):
        def body(offset, carry):
            getattr(make(offset), act)()
            return carry
        lax.fori_loop(1, chips, body, 0)

    each(scatter, "start")
    slots[0] = own[me]
    each(scatter, "wait_recv")
    held[core, me] = jnp.sum(slots[...], axis=0)
    each(gather, "start")
    each(scatter, "wait_send")
    each(gather, "wait_recv")
    last = pltpu.make_async_remote_copy(
        src_ref=held.at[core], dst_ref=held.at[core], send_sem=last_sems.at[0], recv_sem=last_sems.at[1],
        device_id=mate, device_id_type=MESH)
    last.start()
    each(gather, "wait_send")
    last.wait()
    out_ref[...] = held[...]


def device_sum(value, axes):
    sizes = tuple(lax.axis_size(axis) for axis in axes)
    chips = sizes[0] * sizes[1] // 2
    height, width = value.shape
    piece = height // (2 * chips)
    shape = (2, chips, piece, width)
    f32 = jnp.float32
    out = pl.pallas_call(
        functools.partial(sum_kernel, axes, sizes),
        out_shape=jax.ShapeDtypeStruct(shape, f32),
        in_specs=[pl.BlockSpec(memory_space=pltpu.VMEM)],
        out_specs=pl.BlockSpec(memory_space=pltpu.VMEM),
        scratch_shapes=[
            pltpu.VMEM((chips, piece, width), f32),
            pltpu.VMEM((chips, piece, width), f32),
            pltpu.VMEM((chips, piece, width), f32),
            pltpu.VMEM(shape, f32),
            pltpu.SemaphoreType.DMA((2,)),
            pltpu.SemaphoreType.DMA((2, chips)),
            pltpu.SemaphoreType.DMA((2, chips)),
            pltpu.SemaphoreType.DMA((2,)),
        ],
        compiler_params=pltpu.CompilerParams(collective_id=0, has_side_effects=True),
        name="device_sum",
    )(value.reshape(shape))
    return out.reshape(height, width)


def project_kernel(per_step, columns_ref, blocks_ref, basis_ref, *refs):
    *parts, out_ref, window_ref, sems = refs
    step = pl.program_id(0)
    stored, block_len = blocks_ref.shape[1], blocks_ref.shape[2]

    @pl.when(step == 0)
    def _():
        out_ref[...] = jnp.zeros_like(out_ref)
        copies, at = [], 0
        for index, part in enumerate(parts):
            size = part.shape[0]
            copies.append(pltpu.make_async_copy(part, window_ref.at[pl.ds(at, size)], sems.at[index]))
            at += size
        for copy in copies:
            copy.start()
        for copy in copies:
            copy.wait()

    images = []
    for r in range(per_step):
        picked = []
        for j in range(stored):
            at = columns_ref[step * per_step + r, j] * block_len
            picked.append(window_ref[pl.ds(pl.multiple_of(at, block_len), block_len), :])
        left = jnp.concatenate([blocks_ref[r, j] for j in range(stored)], axis=1)
        right = jnp.concatenate(picked, axis=0)
        images.append(jnp.dot(left, right, preferred_element_type=jnp.float32))
    image = jnp.concatenate(images, axis=0)
    image_high, image_low = split(image)
    basis_high, basis_low = split(basis_ref[...])
    rows = ((0,), (0,))
    term = dot(basis_high, image_high, rows, None)
    term = term + dot(basis_high, image_low, rows, None)
    term = term + dot(basis_low, image_high, rows, None)
    out_ref[...] += term


def project(columns, blocks, basis, parts):
    block_rows, stored, block_len, _ = blocks.shape
    width = basis.shape[1]
    per_step = 2
    depth = sum(part.shape[0] for part in parts)
    grid_spec = pltpu.PrefetchScalarGridSpec(
        num_scalar_prefetch=1,
        grid=(block_rows // per_step,),
        in_specs=[
            pl.BlockSpec((per_step, stored, block_len, block_len), lambda i, c: (i, 0, 0, 0)),
            pl.BlockSpec((per_step * block_len, width), lambda i, c: (i, 0)),
        ] + [pl.BlockSpec(memory_space=pl.ANY)] * len(parts),
        out_specs=pl.BlockSpec((width, width), lambda i, c: (0, 0)),
        scratch_shapes=[
            pltpu.VMEM((depth, width), jnp.bfloat16),
            pltpu.SemaphoreType.DMA((len(parts),)),
        ],
    )
    return pl.pallas_call(
        functools.partial(project_kernel, per_step),
        grid_spec=grid_spec,
        out_shape=jax.ShapeDtypeStruct((width, width), jnp.float32),
        compiler_params=pltpu.CompilerParams(vmem_limit_bytes=40 * 2**20),
        name="project",
    )(columns, blocks, basis, *parts)


def ring(value, axis):
    size = lax.axis_size(axis)
    for shift in range(1, size):
        yield lax.ppermute(value, axis, [((d + shift) % size, d) for d in range(size)])


def local(snapshots, blocks, columns):
    axes = ("rows", "grp")
    height = snapshots.shape[0]
    early = height // 2
    raws = list(ring(snapshots[:early], "grp"))
    gram = device_sum(dot(snapshots, snapshots, ((0,), (0,))), axes)
    factor, inverse = factorize(gram)
    basis = dot(snapshots, inverse)
    basis_half = basis.astype(jnp.bfloat16)
    lates = list(ring(basis_half[early:], "grp"))
    parts = [basis_half]
    for raw, late in zip(raws, lates):
        parts += [dot(raw, inverse).astype(jnp.bfloat16), late]
    block_rows = blocks.shape[0]
    size = lax.axis_size("grp")
    turned = lax.rem(columns + (size - lax.axis_index("grp")) * block_rows, size * block_rows)
    projected = device_sum(project(turned, blocks, basis, parts), axes)
    total_rows = height * lax.axis_size(axes)
    return projected, factor / math.sqrt(total_rows)


def solution(mesh):
    return jax.shard_map(
        local,
        mesh=mesh,
        in_specs=(
            P(("rows", "grp"), None),
            P(("rows", "grp"), None, None, None),
            P(("rows", "grp"), None),
        ),
        out_specs=(P(), P()),
        check_vma=False,
    )
```

profile of v0, /device:TPU:0, one launch (start us, length us, event | category | flops | bytes accessed | tf_op | source)
XLA Modules:
  0.0 148.6 jit_solution(4975792432313233282)
XLA Ops:
  0.6 0.0 copy-start.4
  0.6 3.2 %slice.6 = f32[2048,256]{1,0:T(8,128)} slice(f32[4096,256]{1,0:T(8,128)} %param.3), slice={[0:2048], [0:256]} | slice | bytes 4194304 | tf_op jit(solution)/shard_map/slice | solution.py:295
  3.8 3.0 %collective-permute-start = (f32[2048,256]{1,0:T(8,128)}, f32[2048,256]{1,0:T(8,128)}, u32[]{:S(2)}, u32[]{:S(2)}) collective-permute-start(f32[2048,256]{1,0:T(8,128)} %slice.6), channel_id=1, source_target_pairs={{1,0},{0,1},{3,2},{2,3},{5,4},{4,5},{7,6},{6,7},{9,8},{8,9},{11,10... | collective-permute-start | bytes 6291464 | tf_op jit(solution)/shard_map/ppermute | solution.py:288
  6.8 0.0 copy-done.4
  6.8 7.5 %fusion.3 = f32[256,256]{1,0:T(8,128)} fusion(f32[4096,256]{1,0:T(8,128)S(1)} %copy-done.4), kind=kOutput, calls=%fused_computation.8 | convolution fusion | flops 3221225472 | bytes 4456448 | tf_op jit(solution)/shard_map/dot_general | solution.py:18
  14.3 49.5 %device_sum.2 = f32[2,16,8,256]{3,2,1,0:T(8,128)} custom-call(f32[2,16,8,256]{3,2,1,0:T(8,128)} %bitcast.16), custom_call_target="tpu_custom_call" | custom-call | tf_op jit(solution)/shard_map/device_sum/pallas_call | solution.py:200
  63.8 0.0 copy-start.2
  63.9 0.9 copy-done.2
  64.8 9.8 %factorize.1 = (f32[256,256]{1,0:T(8,128)S(1)}, f32[256,256]{1,0:T(8,128)S(1)}) custom-call(f32[256,256]{1,0:T(8,128)S(1)} %bitcast.15), custom_call_target="tpu_custom_call" | custom-call | tf_op jit(solution)/shard_map/factorize/pallas_call | solution.py:110
  74.6 0.0 copy-start.3
  74.6 0.0 copy-start.5
  74.6 7.7 %fusion.2 = (bf16[4096,256]{1,0:T(8,128)(2,1)S(1)}, f32[4096,256]{1,0:T(8,128)}) fusion(f32[256,256]{1,0:T(8,128)S(1)} %get-tuple-element.4, f32[4096,256]{1,0:T(8,128)} %param.3), kind=kOutput, calls=%fused_computation.7 | convolution fusion | flops 3222274048 | bytes 10747904 | tf_op jit(solution)/shard_map/dot_general | solution.py:18
  82.3 0.0 copy-done.3
  82.3 1.1 slice.8
  83.4 0.7 collective-permute-start.1
  84.1 0.0 copy-done.5
  84.1 0.1 copy.5
  84.1 1.7 %broadcast_multiply_fusion = f32[256,256]{1,0:T(8,128)} fusion(f32[256,256]{1,0:T(8,128)} %copy-done.3), kind=kLoop, calls=%fused_computation.3 | loop fusion | flops 65536 | bytes 524288 | tf_op jit(solution)/shard_map/div | solution.py:309
  85.8 0.0 collective-permute-done
  85.8 3.7 %fusion.refs_1_ = bf16[2048,256]{1,0:T(8,128)(2,1)S(1)} fusion(f32[256,256]{1,0:T(8,128)S(1)} %get-tuple-element.4, f32[2048,256]{1,0:T(8,128)} %collective-permute-done), kind=kOutput, calls=%fused_computation.2 | convolution fusion | flops 1611137024 | bytes 3407872 | tf_op jit(solution)/shard_map/dot_general | solution.py:18
  89.5 19.5 %collective-permute-done.1.refs_2_ = bf16[2048,256]{1,0:T(8,128)(2,1)S(1)} collective-permute-done((bf16[2048,256]{1,0:T(8,128)(2,1)}, bf16[2048,256]{1,0:T(8,128)(2,1)S(1)}, u32[]{:S(2)}, u32[]{:S(2)}) %collective-permute-start.1) | collective-permute-done | bytes 1048608 | tf_op jit(solution)/shard_map/ppermute | solution.py:288
  109.0 0.0 copy-start
  109.0 2.2 %copy-done = f32[4096,256]{1,0:T(8,128)S(1)} copy-done((f32[4096,256]{1,0:T(8,128)S(1)}, f32[4096,256]{1,0:T(8,128)}, u32[]{:S(2)}) %copy-start) | copy-done | bytes 4194328
  111.2 18.3 %project.1 = f32[256,256]{1,0:T(8,128)S(1)} custom-call(s32[32,16]{1,0:T(8,128)S(1)} %negate_select_fusion.columns_ref, bf16[32,16,128,128]{3,2,1,0:T(8,128)(2,1)} %blocks_ref.1, f32[4096,256]{1,0:T(8,128)S(1)} %copy-done, bf16[4096,256]{1,0:T(8,128)(2,1)S(1)} %get-tuple-element.6.refs_0_, bf16[2048,256]{1,0:T(8,128)(2,1)S(1)} %fusion.refs_1_, ...), custom_call_target="tpu_custom_call" | custom-call | tf_op jit(solution)/shard_map/project/pallas_call | solution.py:276
  129.5 0.0 copy-start.1
  129.5 0.7 copy-done.1
  130.2 16.7 %device_sum.3 = f32[2,16,8,256]{3,2,1,0:T(8,128)} custom-call(f32[2,16,8,256]{3,2,1,0:T(8,128)} %bitcast.14), custom_call_target="tpu_custom_call" | custom-call | tf_op jit(solution)/shard_map/device_sum/pallas_call | solution.py:200
  146.9 1.7 %copy.11 = f32[256,256]{1,0:T(8,128)} copy(f32[256,256]{1,0:T(8,128)} %bitcast.17) | data formatting | bytes 524288
  (1 shorter events, 0.0 us)
Async XLA Ops:
  0.6 6.2 %copy-start.4 = (f32[4096,256]{1,0:T(8,128)S(1)}, f32[4096,256]{1,0:T(8,128)}, u32[]{:S(2)}) copy-start(f32[4096,256]{1,0:T(8,128)} %param.3) | copy-start | bytes 12582916
  3.8 82.0 %collective-permute-start = (f32[2048,256]{1,0:T(8,128)}, f32[2048,256]{1,0:T(8,128)}, u32[]{:S(2)}, u32[]{:S(2)}) collective-permute-start(f32[2048,256]{1,0:T(8,128)} %slice.6), channel_id=1, source_target_pairs={{1,0},{0,1},{3,2},{2,3},{5,4},{4,5},{7,6},{6,7},{9,8},{8,9},{11,10... | collective-permute-start | bytes 6291464 | tf_op jit(solution)/shard_map/ppermute | solution.py:288
  63.8 1.0 copy-start.2
  74.6 7.7 %copy-start.3 = (f32[256,256]{1,0:T(8,128)}, f32[256,256]{1,0:T(8,128)S(1)}, u32[]{:S(2)}) copy-start(f32[256,256]{1,0:T(8,128)S(1)} %get-tuple-element.5) | copy-start | bytes 786436
  74.6 9.5 %copy-start.5 = (s32[32,16]{0,1:T(8,128)S(1)}, s32[32,16]{0,1:T(8,128)}, u32[]{:S(2)}) copy-start(s32[32,16]{0,1:T(8,128)} %param.5) | copy-start | bytes 6148
  83.4 25.6 %collective-permute-start.1 = (bf16[2048,256]{1,0:T(8,128)(2,1)}, bf16[2048,256]{1,0:T(8,128)(2,1)S(1)}, u32[]{:S(2)}, u32[]{:S(2)}) collective-permute-start(bf16[2048,256]{1,0:T(8,128)(2,1)} %slice.8), channel_id=1, source_target_pairs={{1,0},{0,1},{3,2},{2,3},{5,4},{4,5},{7,6},{6,7},{9,8},{8,9},{11,10... | collective-permute-start | bytes 3145736 | tf_op jit(solution)/shard_map/ppermute | solution.py:288
  109.0 2.2 %copy-start = (f32[4096,256]{1,0:T(8,128)S(1)}, f32[4096,256]{1,0:T(8,128)}, u32[]{:S(2)}) copy-start(f32[4096,256]{1,0:T(8,128)} %get-tuple-element.7.basis_ref) | copy-start | bytes 12582916
  129.5 0.7 copy-start.1
where the time goes:
time: 149 us
  Pallas kernels  94.3 us (63%)
  waiting for transfers between devices  19.5 us (13%)
  matrix products  18.8 us (13%)
  local copies, waits for them, and re-layouts  9.91 us (7%)
  starting transfers between devices  3.63 us (2%)
  other arithmetic  1.69 us (1%)
    pallas_call x2, Pallas kernels, device_sum(): pl.pallas_call(functools.partial(sum_kernel, axes, sizes), out_shape=jax....  66.2 us
    ppermute x2, waiting for transfers between devices, ring(): lax.ppermute(value, axis, [((d + shift) % size, d) for d in range(size)])  19.5 us
    dot_general x3, matrix products, dot(): lax.dot_general(left, right, (dims, ((), ())), precision=precision, prefe...  18.8 us
    pallas_call x1, Pallas kernels, project(): pl.pallas_call(functools.partial(project_kernel, per_step), grid_spec=gri...  18.3 us
    pallas_call x1, Pallas kernels, factorize(): pl.pallas_call(factor_kernel, out_shape=(square, square), in_specs=[pl.Bl...  9.77 us
    unnamed x14, local copies, waits for them, and re-layouts  5.59 us
    ppermute x2, starting transfers between devices, ring(): lax.ppermute(value, axis, [((d + shift) % size, d) for d in range(size)])  3.63 us
    slice x1, local copies, waits for them, and re-layouts, local(): raws = list(ring(snapshots[:early], 'grp'))  3.2 us
  transfers between devices with their start and end apart: 2, of which 1 were waited for; matrix products, arithmetic and copies ran while one was open for 15% of the time, Pallas kernels for 40%

commit v1 on v0

--- a/solution.py
+++ b/solution.py
@@ -123,36 +123,98 @@
     return high, (value - high.astype(jnp.float32)).astype(jnp.bfloat16)
 
 
-def sum_kernel(axes, sizes, x_ref, out_ref, pair, own, slots, held, pair_sems, scatter_sems, gather_sems, last_sems):
-    rows_axis, grp_axis = axes
-    grps = sizes[1]
-    chips = x_ref.shape[1]
-    me_row, me_grp = lax.axis_index(rows_axis), lax.axis_index(grp_axis)
+def mate_of(axes):
+    row = lax.axis_index(axes[0])
+    return {axes[0]: row + 1 - 2 * lax.rem(row, 2), axes[1]: lax.axis_index(axes[1])}
+
+
+def greet(barrier, where):
+    pl.semaphore_signal(barrier, inc=1, device_id=where, device_id_type=MESH)
+
+
+def exchange(source, target, sems, where):
+    return pltpu.make_async_remote_copy(
+        src_ref=source, dst_ref=target, send_sem=sems.at[0], recv_sem=sems.at[1],
+        device_id=where, device_id_type=MESH)
+
+
+def near_kernel(axes, grps, x_ref, out_ref, pair, own, others, pair_sems, grp_sems):
+    me_row, me_grp = lax.axis_index(axes[0]), lax.axis_index(axes[1])
     core = lax.rem(me_row, 2)
-    me = (me_row // 2) * grps + me_grp
-
-    def chip(offset):
-        other = lax.rem(me + offset, chips)
-        return other, {rows_axis: (other // grps) * 2 + core, grp_axis: lax.rem(other, grps)}
-
-    mate = {rows_axis: me_row + 1 - 2 * core, grp_axis: me_grp}
-
+    mate = mate_of(axes)
+    friends = [{axes[0]: me_row, axes[1]: lax.rem(me_grp + shift, grps)} for shift in range(1, grps)]
     barrier = pltpu.get_barrier_semaphore()
-    pl.semaphore_signal(barrier, inc=1, device_id=mate, device_id_type=MESH)
-
-    def greet(offset, carry):
-        pl.semaphore_signal(barrier, inc=1, device_id=chip(offset)[1], device_id_type=MESH)
-        return carry
-
-    lax.fori_loop(1, chips, greet, 0)
-    pl.semaphore_wait(barrier, chips)
-
-    first = pltpu.make_async_remote_copy(
-        src_ref=x_ref.at[1 - core], dst_ref=pair, send_sem=pair_sems.at[0], recv_sem=pair_sems.at[1],
-        device_id=mate, device_id_type=MESH)
+    for where in [mate] + friends:
+        greet(barrier, where)
+    pl.semaphore_wait(barrier, grps)
+    first = exchange(x_ref.at[1 - core], pair, pair_sems, mate)
     first.start()
     first.wait()
     own[...] = x_ref[core] + pair[...]
+    copies = [exchange(own, others.at[i], grp_sems.at[i], where) for i, where in enumerate(friends)]
+    for copy in copies:
+        copy.start()
+    total = own[...]
+    for i, copy in enumerate(copies):
+        copy.wait()
+        total = total + others[i]
+    out_ref[...] = total
+
+
+def near_sum(value, axes, chips):
+    height, width = value.shape
+    grps = lax.axis_size(axes[1])
+    half = (chips, height // (2 * chips), width)
+    f32 = jnp.float32
+    return pl.pallas_call(
+        functools.partial(near_kernel, axes, grps),
+        out_shape=jax.ShapeDtypeStruct(half, f32),
+        in_specs=[pl.BlockSpec(memory_space=pltpu.VMEM)],
+        out_specs=pl.BlockSpec(memory_space=pltpu.VMEM),
+        scratch_shapes=[
+            pltpu.VMEM(half, f32),
+            pltpu.VMEM(half, f32),
+            pltpu.VMEM((grps - 1,) + half, f32),
+            pltpu.SemaphoreType.DMA((2,)),
+            pltpu.SemaphoreType.DMA((grps - 1, 2)),
+        ],
+        compiler_params=pltpu.CompilerParams(collective_id=1, has_side_effects=True),
+        name="near_sum",
+    )(value.reshape((2,) + half))
+
+
+def sum_kernel(axes, grps, x_ref, out_ref, pair, own, slots, held, pair_sems, scatter_sems, gather_sems, last_sems):
+    rows_axis, grp_axis = axes
+    chips = own.shape[0]
+    me_row, me_grp = lax.axis_index(rows_axis), lax.axis_index(grp_axis)
+    core = lax.rem(me_row, 2)
+    mate = mate_of(axes)
+    whole = grps > 1
+    me = (me_row // 2) * grps + me_grp if whole else me_row // 2
+
+    def chip(offset):
+        other = lax.rem(me + offset, chips)
+        if whole:
+            return other, {rows_axis: (other // grps) * 2 + core, grp_axis: lax.rem(other, grps)}
+        return other, {rows_axis: other * 2 + core, grp_axis: me_grp}
+
+    barrier = pltpu.get_barrier_semaphore()
+    greet(barrier, mate)
+
+    def greet_chip(offset, carry):
+        greet(barrier, chip(offset)[1])
+        return carry
+
+    lax.fori_loop(1, chips, greet_chip, 0, unroll=chips <= 16)
+    pl.semaphore_wait(barrier, chips)
+
+    if whole:
+        first = exchange(x_ref.at[1 - core], pair, pair_sems, mate)
+        first.start()
+        first.wait()
+        own[...] = x_ref[core] + pair[...]
+    else:
+        own[...] = x_ref[...]
 
     def scatter(offset):
         other, where = chip(offset)
@@ -172,7 +234,7 @@
         def body(offset, carry):
             getattr(make(offset), act)()
             return carry
-        lax.fori_loop(1, chips, body, 0)
+        lax.fori_loop(1, chips, body, 0, unroll=chips <= 16)
 
     each(scatter, "start")
     slots[0] = own[me]
@@ -181,41 +243,90 @@
     each(gather, "start")
     each(scatter, "wait_send")
     each(gather, "wait_recv")
-    last = pltpu.make_async_remote_copy(
-        src_ref=held.at[core], dst_ref=held.at[core], send_sem=last_sems.at[0], recv_sem=last_sems.at[1],
-        device_id=mate, device_id_type=MESH)
+    last = exchange(held.at[core], held.at[core], last_sems, mate)
     last.start()
     each(gather, "wait_send")
     last.wait()
     out_ref[...] = held[...]
 
 
-def device_sum(value, axes):
-    sizes = tuple(lax.axis_size(axis) for axis in axes)
-    chips = sizes[0] * sizes[1] // 2
-    height, width = value.shape
-    piece = height // (2 * chips)
-    shape = (2, chips, piece, width)
+def device_sum(value, axes, whole=True):
+    grps = lax.axis_size(axes[1]) if whole else 1
+    chips = lax.axis_size(axes[0]) // 2 * grps
+    height, width = (value.shape[0], value.shape[1]) if whole else (2 * chips * value.shape[1], value.shape[2])
+    half = (chips, height // (2 * chips), width)
     f32 = jnp.float32
     out = pl.pallas_call(
-        functools.partial(sum_kernel, axes, sizes),
-        out_shape=jax.ShapeDtypeStruct(shape, f32),
+        functools.partial(sum_kernel, axes, grps),
+        out_shape=jax.ShapeDtypeStruct((2,) + half, f32),
         in_specs=[pl.BlockSpec(memory_space=pltpu.VMEM)],
         out_specs=pl.BlockSpec(memory_space=pltpu.VMEM),
         scratch_shapes=[
-            pltpu.VMEM((chips, piece, width), f32),
-            pltpu.VMEM((chips, piece, width), f32),
-            pltpu.VMEM((chips, piece, width), f32),
-            pltpu.VMEM(shape, f32),
+            pltpu.VMEM(half, f32),
+            pltpu.VMEM(half, f32),
+            pltpu.VMEM(half, f32),
+            pltpu.VMEM((2,) + half, f32),
             pltpu.SemaphoreType.DMA((2,)),
             pltpu.SemaphoreType.DMA((2, chips)),
             pltpu.SemaphoreType.DMA((2, chips)),
             pltpu.SemaphoreType.DMA((2,)),
         ],
-        compiler_params=pltpu.CompilerParams(collective_id=0, has_side_effects=True),
-        name="device_sum",
-    )(value.reshape(shape))
+        compiler_params=pltpu.CompilerParams(collective_id=0 if whole else 2, has_side_effects=True),
+        name="device_sum" if whole else "far_sum",
+    )(value.reshape((2,) + half) if whole else value)
     return out.reshape(height, width)
+
+
+def gram_kernel(early_tiles, s_ref, out_ref, raw_ref, cross_ref):
+    step = pl.program_id(0)
+    value = s_ref[...]
+    high = value.astype(jnp.bfloat16)
+    rest = value - high.astype(jnp.float32)
+    mid = rest.astype(jnp.bfloat16)
+    low = (rest - mid.astype(jnp.float32)).astype(jnp.bfloat16)
+    rows = ((0,), (0,))
+    square = dot(high, high, rows, None) + dot(mid, mid, rows, None)
+    cross = dot(high, mid, rows, None) + dot(high, low, rows, None)
+
+    @pl.when(step == 0)
+    def _():
+        out_ref[...] = square
+        cross_ref[...] = cross
+
+    @pl.when(step > 0)
+    def _():
+        out_ref[...] += square
+        cross_ref[...] += cross
+
+    @pl.when(step < early_tiles)
+    def _():
+        raw_ref[...] = value
+
+    @pl.when(step == pl.num_programs(0) - 1)
+    def _():
+        cross = cross_ref[...]
+        out_ref[...] += cross + cross.T
+
+
+def gram_of(snapshots, early, tile=512):
+    height, width = snapshots.shape
+    early_tiles = early // tile
+    return pl.pallas_call(
+        functools.partial(gram_kernel, early_tiles),
+        grid=(height // tile,),
+        in_specs=[pl.BlockSpec((tile, width), lambda i: (i, 0))],
+        out_specs=(
+            pl.BlockSpec((width, width), lambda i: (0, 0)),
+            pl.BlockSpec((tile, width), lambda i: (jnp.minimum(i, early_tiles - 1), 0)),
+        ),
+        out_shape=(
+            jax.ShapeDtypeStruct((width, width), jnp.float32),
+            jax.ShapeDtypeStruct((early, width), jnp.float32),
+        ),
+        scratch_shapes=[pltpu.VMEM((width, width), jnp.float32)],
+        compiler_params=pltpu.CompilerParams(vmem_limit_bytes=16 * 2**20),
+        name="gram",
+    )(snapshots)
 
 
 def project_kernel(per_step, columns_ref, blocks_ref, basis_ref, *refs):
@@ -291,16 +402,22 @@
 def local(snapshots, blocks, columns):
     axes = ("rows", "grp")
     height = snapshots.shape[0]
-    early = height // 2
-    raws = list(ring(snapshots[:early], "grp"))
-    gram = device_sum(dot(snapshots, snapshots, ((0,), (0,))), axes)
-    factor, inverse = factorize(gram)
-    basis = dot(snapshots, inverse)
+    early = height // 4
+    gram, raw = gram_of(snapshots, early)
+    near = near_sum(gram, axes, lax.axis_size("rows") // 2)
+    near, raw = lax.optimization_barrier((near, raw))
+    raws = list(ring(raw, "grp"))
+    factor, inverse = factorize(device_sum(near, axes, whole=False))
+    cuts = (early, early + height // 4, height)
+    pieces, lates = [], []
+    for start, stop in zip(cuts[:-1], cuts[1:]):
+        pieces.append(dot(snapshots[start:stop], inverse))
+        lates.append(list(ring(pieces[-1].astype(jnp.bfloat16), "grp")))
+    basis = jnp.concatenate([dot(snapshots[:early], inverse)] + pieces, axis=0)
     basis_half = basis.astype(jnp.bfloat16)
-    lates = list(ring(basis_half[early:], "grp"))
     parts = [basis_half]
-    for raw, late in zip(raws, lates):
-        parts += [dot(raw, inverse).astype(jnp.bfloat16), late]
+    for index, raw in enumerate(raws):
+        parts += [dot(raw, inverse).astype(jnp.bfloat16)] + [late[index] for late in lates]
     block_rows = blocks.shape[0]
     size = lax.axis_size("grp")
     turned = lax.rem(columns + (size - lax.axis_index("grp")) * block_rows, size * block_rows)

time: 149 us -> 125 us (0.84)
  Pallas kernels: 94.3 us -> 75.4 us
  matrix products: 18.8 us -> 12.3 us
  other arithmetic: 1.69 us -> 5.51 us
  local copies, waits for them, and re-layouts: 9.91 us -> 6.29 us
    pallas_call x2 -> x4, Pallas kernels: 66.2 us -> 47.4 us  [the longest x2 33 us: device_sum(): pl.pallas_call(functools.partial(sum_kernel, axes, grps), out_shape=jax.S...]
    dot_general x3 -> x4, matrix products: 18.8 us -> 12.3 us  [dot(): lax.dot_general(left, right, (dims, ((), ())), precision=precision, prefe...]
    slice x2 -> x0, local copies, waits for them, and re-layouts: 4.32 us -> none  [the longest x1 3.2 us: local(): raws = list(ring(snapshots[:early], 'grp'))]
    convert_element_type x0 -> x1, other arithmetic: none -> 2.53 us  [local(): basis_half = basis.astype(jnp.bfloat16)]
    concatenate x0 -> x1, other arithmetic: none -> 2.25 us  [local(): basis = jnp.concatenate([dot(snapshots[:early], inverse)] + pieces, axis=0)]
    unnamed x14 -> x20, local copies, waits for them, and re-layouts: 5.59 us -> 6.29 us
    ppermute x2 -> x3, waiting for transfers between devices: 19.5 us -> 20 us  [ring(): lax.ppermute(value, axis, [((d + shift) % size, d) for d in range(size)])]
    ppermute x2 -> x3, starting transfers between devices: 3.63 us -> 3.98 us  [ring(): lax.ppermute(value, axis, [((d + shift) % size, d) for d in range(size)])]
  transfers between devices with their start and end apart: 2 -> 3, of which waited for: 1 -> 1; matrix products, arithmetic and copies ran while one was open for 15% -> 14% of each run, Pallas kernels for 40% -> 21%
where the time goes in v1:
time: 125 us; the launch traced here: 124 us
  Pallas kernels  75.4 us (60%)
  waiting for transfers between devices  20 us (16%)
  matrix products  12.3 us (10%)
  local copies, waits for them, and re-layouts  6.29 us (5%)
  other arithmetic  5.51 us (4%)
  starting transfers between devices  3.98 us (3%)
    pallas_call x2, Pallas kernels, device_sum(): pl.pallas_call(functools.partial(sum_kernel, axes, grps), out_shape=jax.S...  33 us
    ppermute x3, waiting for transfers between devices, ring(): lax.ppermute(value, axis, [((d + shift) % size, d) for d in range(size)])  20 us
    pallas_call x1, Pallas kernels, project(): pl.pallas_call(functools.partial(project_kernel, per_step), grid_spec=gri...  18.3 us
    dot_general x4, matrix products, dot(): lax.dot_general(left, right, (dims, ((), ())), precision=precision, prefe...  12.3 us
    pallas_call x1, Pallas kernels, near_sum(): pl.pallas_call(functools.partial(near_kernel, axes, grps), out_shape=jax....  9.78 us
    pallas_call x1, Pallas kernels, factorize(): pl.pallas_call(factor_kernel, out_shape=(square, square), in_specs=[pl.Bl...  9.77 us
    unnamed x20, local copies, waits for them, and re-layouts  6.29 us
    pallas_call x1, Pallas kernels, gram_of(): pl.pallas_call(functools.partial(gram_kernel, early_tiles), grid=(height...  4.59 us
  transfers between devices with their start and end apart: 3, of which 1 were waited for; matrix products, arithmetic and copies ran while one was open for 14% of the time, Pallas kernels for 21%

profile of v1, /device:TPU:0, one launch (start us, length us, event | category | flops | bytes accessed | tf_op | source)
XLA Modules:
  0.0 124.2 jit_solution(13630080703461344094)
XLA Ops:
  0.6 0.0 copy-start
  0.6 2.2 %copy-done = f32[4096,256]{1,0:T(8,128)S(1)} copy-done((f32[4096,256]{1,0:T(8,128)S(1)}, f32[4096,256]{1,0:T(8,128)}, u32[]{:S(2)}) %copy-start) | copy-done | bytes 4194328
  2.8 4.6 %gram.1 = (f32[256,256]{1,0:T(8,128)S(1)}, f32[1024,256]{1,0:T(8,128)S(1)}) custom-call(f32[4096,256]{1,0:T(8,128)S(1)} %copy-done), custom_call_target="tpu_custom_call" | custom-call | tf_op jit(solution)/shard_map/gram/pallas_call | solution.py:314
  7.4 0.0 copy-start.4
  7.4 0.7 copy-done.4
  8.1 9.8 %near_sum.1.x_ref = f32[8,16,256]{2,1,0:T(8,128)} custom-call(f32[2,8,16,256]{3,2,1,0:T(8,128)} %bitcast.17), custom_call_target="tpu_custom_call" | custom-call | tf_op jit(solution)/shard_map/near_sum/pallas_call | solution.py:169
  17.9 1.9 %collective-permute-start = (f32[1024,256]{1,0:T(8,128)S(1)}, f32[1024,256]{1,0:T(8,128)}, u32[]{:S(2)}, u32[]{:S(2)}) collective-permute-start(f32[1024,256]{1,0:T(8,128)S(1)} %get-tuple-element.12), channel_id=1, source_target_pairs={{1,0},{0,1},{3,2},{2,3},{5,4},{4,5},{7,6},{6,7},{9,8},{8,9},{11,10... | collective-permute-start | bytes 3145736 | tf_op jit(solution)/shard_map/ppermute | solution.py:399
  19.9 16.6 %far_sum.1 = f32[2,8,16,256]{3,2,1,0:T(8,128)} custom-call(f32[8,16,256]{2,1,0:T(8,128)} %near_sum.1.x_ref), custom_call_target="tpu_custom_call" | custom-call | tf_op jit(solution)/shard_map/far_sum/pallas_call | solution.py:259
  36.5 0.0 copy-start.3
  36.5 0.9 copy-done.3
  37.4 9.8 %factorize.1 = (f32[256,256]{1,0:T(8,128)S(1)}, f32[256,256]{1,0:T(8,128)S(1)}) custom-call(f32[256,256]{1,0:T(8,128)S(1)} %bitcast.16), custom_call_target="tpu_custom_call" | custom-call | tf_op jit(solution)/shard_map/factorize/pallas_call | solution.py:110
  47.2 3.1 %fusion.5 = (bf16[1024,256]{1,0:T(8,128)(2,1)}, f32[1024,256]{1,0:T(8,128)S(1)}) fusion(f32[256,256]{1,0:T(8,128)S(1)} %get-tuple-element.11, f32[4096,256]{1,0:T(8,128)} %s_ref.1), kind=kOutput, calls=%fused_computation.13 | convolution fusion | flops 805568512 | bytes 2883584 | tf_op jit(solution)/shard_map/dot_general | solution.py:18
  50.3 0.5 collective-permute-start.1
  50.8 4.5 %fusion.6 = (bf16[2048,256]{1,0:T(8,128)(2,1)}, f32[2048,256]{1,0:T(8,128)S(1)}) fusion(f32[256,256]{1,0:T(8,128)S(1)} %get-tuple-element.11, f32[4096,256]{1,0:T(8,128)} %s_ref.1), kind=kOutput, calls=%fused_computation.14 | convolution fusion | flops 1611137024 | bytes 5505024 | tf_op jit(solution)/shard_map/dot_general | solution.py:18
  55.3 1.5 %collective-permute-start.2 = (bf16[2048,256]{1,0:T(8,128)(2,1)}, bf16[2048,256]{1,0:T(8,128)(2,1)S(1)}, u32[]{:S(2)}, u32[]{:S(2)}) collective-permute-start(bf16[2048,256]{1,0:T(8,128)(2,1)} %get-tuple-element.16), channel_id=1, source_target_pairs={{1,0},{0,1},{3,2},{2,3},{5,4},{4,5},{7,6},{6,7},{9,8},{8,9},{11,10... | collective-permute-start | bytes 3145736 | tf_op jit(solution)/shard_map/ppermute | solution.py:399
  56.8 2.4 %convolution_bitcast_fusion.2 = f32[1024,256]{1,0:T(8,128)S(1)} fusion(f32[256,256]{1,0:T(8,128)S(1)} %get-tuple-element.11, f32[4096,256]{1,0:T(8,128)} %s_ref.1), kind=kOutput, calls=%fused_computation.4 | convolution fusion | flops 805306368 | bytes 2359296 | tf_op jit(solution)/shard_map/dot_general | solution.py:18
  59.3 0.0 copy-start.8
  59.3 2.2 %pad_maximum_fusion.basis_ref = f32[4096,256]{1,0:T(8,128)} fusion(f32[2048,256]{1,0:T(8,128)S(1)} %get-tuple-element.17, f32[1024,256]{1,0:T(8,128)S(1)} %get-tuple-element.15, f32[1024,256]{1,0:T(8,128)S(1)} %convolution_bitcast_fusion.2), kind=kLoop, calls=%fused_computation | loop fusion | flops 2097152 | bytes 8388608 | tf_op jit(solution)/shard_map/concatenate | solution.py:416
  61.5 0.0 copy-done.5
  61.6 0.0 copy-done.8
  61.6 0.1 copy.5
  61.6 2.5 %fusion.4.refs_0_ = bf16[4096,256]{1,0:T(8,128)(2,1)S(1)} fusion(f32[2048,256]{1,0:T(8,128)} %copy-done.5, f32[1024,256]{1,0:T(8,128)} %copy-done.7, f32[1024,256]{1,0:T(8,128)} %copy-done.6), kind=kLoop, calls=%fused_computation.12 | loop fusion | flops 6291456 | bytes 6291456 | tf_op jit(solution)/shard_map/convert_element_type | solution.py:417
  64.2 0.7 broadcast_multiply_fusion
  64.9 0.0 collective-permute-done
  64.9 2.2 %convolution_convert_fusion.refs_1_ = bf16[1024,256]{1,0:T(8,128)(2,1)S(1)} fusion(f32[1024,256]{1,0:T(8,128)} %collective-permute-done, f32[256,256]{1,0:T(8,128)S(1)} %get-tuple-element.11), kind=kOutput, calls=%fused_computation.5 | convolution fusion | flops 805568512 | bytes 1835008 | tf_op jit(solution)/shard_map/dot_general | solution.py:18
  67.1 0.0 collective-permute-done.1.refs_2_
  67.2 20.0 %collective-permute-done.2.refs_3_ = bf16[2048,256]{1,0:T(8,128)(2,1)S(1)} collective-permute-done((bf16[2048,256]{1,0:T(8,128)(2,1)}, bf16[2048,256]{1,0:T(8,128)(2,1)S(1)}, u32[]{:S(2)}, u32[]{:S(2)}) %collective-permute-start.2) | collective-permute-done | bytes 1048608 | tf_op jit(solution)/shard_map/ppermute | solution.py:399
  87.1 18.3 %project.1 = f32[256,256]{1,0:T(8,128)S(1)} custom-call(s32[32,16]{1,0:T(8,128)S(1)} %negate_select_fusion.columns_ref, bf16[32,16,128,128]{3,2,1,0:T(8,128)(2,1)} %blocks_ref.1, f32[4096,256]{1,0:T(8,128)S(1)} %copy-done.1, bf16[4096,256]{1,0:T(8,128)(2,1)S(1)} %fusion.4.refs_0_, bf16[1024,256]{1,0:T(8,128)(2,1)S(1)} %convolution_convert_fusion.refs_1_, ...), custom_call_target="tpu_custom_call" | custom-call | tf_op jit(solution)/shard_map/project/pallas_call | solution.py:387
  105.5 0.0 copy-start.2
  105.5 0.7 copy-done.2
  106.2 16.4 %device_sum.1 = f32[2,16,8,256]{3,2,1,0:T(8,128)} custom-call(f32[2,16,8,256]{3,2,1,0:T(8,128)} %bitcast.15), custom_call_target="tpu_custom_call" | custom-call | tf_op jit(solution)/shard_map/device_sum/pallas_call | solution.py:259
  122.6 1.7 %copy.13 = f32[256,256]{1,0:T(8,128)} copy(f32[256,256]{1,0:T(8,128)} %bitcast.18) | data formatting | bytes 524288
  (8 shorter events, 0.0 us)
Async XLA Ops:
  0.6 2.2 %copy-start = (f32[4096,256]{1,0:T(8,128)S(1)}, f32[4096,256]{1,0:T(8,128)}, u32[]{:S(2)}) copy-start(f32[4096,256]{1,0:T(8,128)} %s_ref.1) | copy-start | bytes 12582916
  7.4 0.7 copy-start.4
  17.9 47.0 %collective-permute-start = (f32[1024,256]{1,0:T(8,128)S(1)}, f32[1024,256]{1,0:T(8,128)}, u32[]{:S(2)}, u32[]{:S(2)}) collective-permute-start(f32[1024,256]{1,0:T(8,128)S(1)} %get-tuple-element.12), channel_id=1, source_target_pairs={{1,0},{0,1},{3,2},{2,3},{5,4},{4,5},{7,6},{6,7},{9,8},{8,9},{11,10... | collective-permute-start | bytes 3145736 | tf_op jit(solution)/shard_map/ppermute | solution.py:399
  36.5 1.0 copy-start.3
  50.3 11.3 %copy-start.7 = (f32[1024,256]{1,0:T(8,128)}, f32[1024,256]{1,0:T(8,128)S(1)}, u32[]{:S(2)}) copy-start(f32[1024,256]{1,0:T(8,128)S(1)} %get-tuple-element.15) | copy-start | bytes 3145732
  50.3 16.9 %collective-permute-start.1 = (bf16[1024,256]{1,0:T(8,128)(2,1)}, bf16[1024,256]{1,0:T(8,128)(2,1)S(1)}, u32[]{:S(2)}, u32[]{:S(2)}) collective-permute-start(bf16[1024,256]{1,0:T(8,128)(2,1)} %get-tuple-element.14), channel_id=1, source_target_pairs={{1,0},{0,1},{3,2},{2,3},{5,4},{4,5},{7,6},{6,7},{9,8},{8,9},{11,10... | collective-permute-start | bytes 1572872 | tf_op jit(solution)/shard_map/ppermute | solution.py:399
  55.3 6.2 %copy-start.5 = (f32[2048,256]{1,0:T(8,128)}, f32[2048,256]{1,0:T(8,128)S(1)}, u32[]{:S(2)}) copy-start(f32[2048,256]{1,0:T(8,128)S(1)} %get-tuple-element.17) | copy-start | bytes 6291460
  55.3 31.8 %collective-permute-start.2 = (bf16[2048,256]{1,0:T(8,128)(2,1)}, bf16[2048,256]{1,0:T(8,128)(2,1)S(1)}, u32[]{:S(2)}, u32[]{:S(2)}) collective-permute-start(bf16[2048,256]{1,0:T(8,128)(2,1)} %get-tuple-element.16), channel_id=1, source_target_pairs={{1,0},{0,1},{3,2},{2,3},{5,4},{4,5},{7,6},{6,7},{9,8},{8,9},{11,10... | collective-permute-start | bytes 3145736 | tf_op jit(solution)/shard_map/ppermute | solution.py:399
  59.3 2.3 %copy-start.6 = (f32[1024,256]{1,0:T(8,128)}, f32[1024,256]{1,0:T(8,128)S(1)}, u32[]{:S(2)}) copy-start(f32[1024,256]{1,0:T(8,128)S(1)} %convolution_bitcast_fusion.2) | copy-start | bytes 3145732
  59.3 2.3 %copy-start.8 = (s32[32,16]{0,1:T(8,128)S(1)}, s32[32,16]{0,1:T(8,128)}, u32[]{:S(2)}) copy-start(s32[32,16]{0,1:T(8,128)} %param.5) | copy-start | bytes 6148
  61.6 25.5 %copy-start.1 = (f32[4096,256]{1,0:T(8,128)S(1)}, f32[4096,256]{1,0:T(8,128)}, u32[]{:S(2)}) copy-start(f32[4096,256]{1,0:T(8,128)} %pad_maximum_fusion.basis_ref) | copy-start | bytes 12582916
  105.5 0.7 copy-start.2
